TPU v7x, 32 devices: a whole 2x2x4 slice. The times are simulated.
32 devices in a mesh: ctx: 8 (over y, x, core), head: 4 (over z).
Axes of the slice: x: 2, y: 2, z: 4, core: 2. Of those that a mesh axis runs over, the one named last changes fastest.
Arguments:
- attn_q: bfloat16 [4096, 2048], P(('ctx', 'head')), may hold values from -6 to 6
- attn_k: bfloat16 [4096, 2048], P(('ctx', 'head')), may hold values from -6 to 6
- attn_v: bfloat16 [4096, 2048], P(('ctx', 'head')), may hold values from -6 to 6
- step_size: float32 [4, 4096], P('head', 'ctx'), may hold values from 0.05 to 1
- fast_init: float32 [4, 3, 512, 512], P('head'), may hold values from -0.25 to 0.25
- boundary: int32 [1], replicated, may hold values from 1024 to 3071
- window_len: int32 [16], replicated, may hold values from 2 to 128, as said below
Outputs:
- layer_out: bfloat16 [4096, 2048], P('ctx', 'head')
Inputs may be any that keep to these rules, and one draw needn't show every extreme that they name: `window_len`: some attention head has a window of exactly 128.
All inputs are finite; a program needn't handle non-finite values.
Results may differ from a plain program's by a relative error of at most 0.017.
Values may be sent and summed in bfloat16 or wider, within the bound.
A program may use at most 64 MiB of HBM per device.

v0:
```python
import functools
import math

import jax
import jax.numpy as jnp
from jax import lax
from jax.experimental import pallas as pl
from jax.experimental.pallas import tpu as pltpu
from jax.sharding import PartitionSpec as P

AH = 128
WIN = 128
NS_STEPS = 2
LAG = 1
ns_linear = 3.4445
ns_cubic = -4.775
ns_quintic = 2.0315
MESH = pl.DeviceIdType.MESH
F32 = jnp.float32
BF = jnp.bfloat16


def sum_plan(rows, n_bits):
    half = rows // 2
    quarter = half // 2
    offset = half
    transfers = 1
    groups = []
    for order in (list(range(1, n_bits)), list(range(n_bits - 1, 0, -1))):
        size = quarter
        steps = []
        for bit in order:
            halve = size // 2 >= 16
            sent = size // 2 if halve else size
            steps.append((bit, halve, size, sent, offset, transfers))
            offset += sent
            transfers += 1
            size = sent
        groups.append((steps, size))
    back = transfers
    transfers += 2 * (n_bits - 1) + 1
    return groups, offset, back, transfers


def kernel(
    n_ctx, n_head, q_hbm, k_hbm, v_hbm, step_ref, init_hbm, bound_ref, win_ref, out_ref,
    q_all, k_all, v_all, kb, kbt, qb, step_t, w32, wb, pre_g, pre_u, back, hid, tgt, bg, bu, xs, sq, mx,
    grad, attended, res1, sb, rb, red,
    loc_sem, a2a_send, a2a_recv, halo_send, halo_recv, ar_send, ar_recv,
):
    ctx = lax.axis_index("ctx")
    head = lax.axis_index("head")
    n_bits = n_ctx.bit_length() - 1
    tok = q_hbm.shape[0]
    fw = q_all.shape[1]
    count = q_all.shape[0]
    half = fw // 2
    quarter = half // 2
    groups, _, back_at, _ = sum_plan(fw, n_bits)

    def bit_of(b):
        return lax.rem(lax.div(ctx, 1 << b), 2)

    def partner(b):
        return ctx + (1 << b) - 2 * (1 << b) * bit_of(b)

    nxt = lax.rem(ctx + 1, n_ctx)
    prv = lax.rem(ctx + n_ctx - 1, n_ctx)

    barrier = pltpu.get_barrier_semaphore()
    for d in range(1, n_head):
        pl.semaphore_signal(
            barrier, inc=1, device_id={"head": lax.rem(head + d, n_head)}, device_id_type=MESH
        )
    for b in range(n_bits):
        pl.semaphore_signal(barrier, inc=1, device_id={"ctx": partner(b)}, device_id_type=MESH)
    pl.semaphore_signal(barrier, inc=1, device_id={"ctx": nxt}, device_id_type=MESH)
    pl.semaphore_signal(barrier, inc=1, device_id={"ctx": prv}, device_id_type=MESH)

    my_cols = pl.ds(pl.multiple_of(head * fw, fw), fw)

    def own_copy(i, src, dst, first):
        rows = pl.ds(pl.multiple_of(first + head * tok, tok), tok)
        return pltpu.make_async_copy(src.at[:, my_cols], dst.at[rows, :], loc_sem.at[i])

    locals_ = [own_copy(0, k_hbm, k_all, WIN), own_copy(1, v_hbm, v_all, WIN), own_copy(2, q_hbm, q_all, 0)]
    init_copy = pltpu.make_async_copy(init_hbm.at[0], w32, loc_sem.at[3])
    for c in locals_:
        c.start()
    init_copy.start()

    pl.semaphore_wait(barrier, n_head - 1 + n_bits + 2)

    def spread(i, src, dst, first):
        copies = []
        for d in range(1, n_head):
            to = lax.rem(head + d, n_head)
            cols = pl.ds(pl.multiple_of(to * fw, fw), fw)
            rows = pl.ds(pl.multiple_of(first + head * tok, tok), tok)
            copies.append(
                pltpu.make_async_remote_copy(
                    src_ref=src.at[:, cols],
                    dst_ref=dst.at[rows, :],
                    send_sem=a2a_send.at[i, d - 1],
                    recv_sem=a2a_recv.at[i, d - 1],
                    device_id={"head": to},
                    device_id_type=MESH,
                )
            )
        return copies

    k_copies = spread(0, k_hbm, k_all, WIN)
    v_copies = spread(1, v_hbm, v_all, WIN)
    q_copies = spread(2, q_hbm, q_all, 0)
    for c in k_copies + v_copies:
        c.start()
    sent = k_copies + v_copies + q_copies

    for i in range(count // 128):
        wide = jnp.broadcast_to(step_ref[0:1, i * 128 : (i + 1) * 128], (128, 128))
        step_t[i * 128 : (i + 1) * 128, :] = wide.T

    init_copy.wait()
    for m in range(3):
        wb[m] = w32[m].astype(BF)

    def chunks(rows, body, size=64):
        def go(i, carry):
            body(pl.ds(pl.multiple_of(i * size, size), size), i * size)
            return carry

        lax.fori_loop(0, rows // size, go, 0)

    def rms(x):
        return x * lax.rsqrt(jnp.mean(x * x, axis=-1, keepdims=True) + 1e-06)

    def dot(a, b, ca=1, cb=0):
        return lax.dot_general(a, b, (((ca,), (cb,)), ((), ())), preferred_element_type=F32)

    def rms_keys(rows, first):
        kb[rows, :] = rms(k_all[pl.ds(pl.multiple_of(first + WIN, 64), 64), :].astype(F32)).astype(BF)

    def rms_queries(rows, first):
        qb[rows, :] = rms(q_all[rows, :].astype(F32)).astype(BF)

    def inside(first, size, block):
        pos = ctx * count + first + lax.broadcasted_iota(jnp.int32, (size, 128), 0)
        early = pos < bound_ref[0]
        return early if block == 0 else jnp.logical_not(early)

    def make_target(block):
        def body(rows, first):
            col = jnp.where(inside(first, 64, block), step_t[rows, :], 0.0)
            scale = jnp.concatenate([col] * (fw // 128), axis=1)
            v = v_all[pl.ds(pl.multiple_of(first + WIN, 64), 64), :].astype(F32)
            tgt[rows, :] = (v * scale).astype(BF)

        chunks(count, body)

    def make_hidden():
        def body(rows, first):
            g = pre_g[rows, :]
            u = pre_u[rows, :]
            act = g * jax.nn.sigmoid(g)
            hid[rows, :] = (act * u).astype(BF)

        chunks(count, body)

    def make_back(with_hidden):
        def body(rows, first):
            g = pre_g[rows, :]
            u = pre_u[rows, :]
            o = back[rows, :]
            sig = jax.nn.sigmoid(g)
            act = g * sig
            if with_hidden:
                hid[rows, :] = (act * u).astype(BF)
            bg[rows, :] = (o * u * sig * (1.0 + g * (1.0 - sig))).astype(BF)
            bu[rows, :] = (o * act).astype(BF)

        chunks(count, body)

    def ctx_copy(block, m, src, dst, t, bit):
        c = pltpu.make_async_remote_copy(
            src_ref=src,
            dst_ref=dst,
            send_sem=ar_send.at[block, m, t],
            recv_sem=ar_recv.at[block, m, t],
            device_id={"ctx": partner(bit)},
            device_id_type=MESH,
        )
        c.start()
        sent.append(c)
        return c

    def al(x, n):
        return pl.multiple_of(x, n)

    def sum_steps(block, m):
        mine = bit_of(0) * half
        other = half - mine
        state = {}

        def first():
            sb[block, m, 0:half, :] = grad[m, pl.ds(al(other, half), half), :].astype(BF)
            state["c"] = [
                ctx_copy(block, m, sb.at[block, m, pl.ds(0, half)], rb.at[block, m, pl.ds(0, half)], 0, 0)
            ]
            state["base"] = [mine, mine + quarter]

        def land_first():
            state["c"][0].wait_recv()
            rows = pl.ds(al(mine, half), half)
            grad[m, rows, :] = grad[m, rows, :] + rb[block, m, 0:half, :].astype(F32)

        def launch(s):
            state["c"] = []
            for g, (steps, _) in enumerate(groups):
                bit, halve, size, part, off, t = steps[s]
                base = state["base"][g]
                if halve:
                    src = base + (1 - bit_of(bit)) * part
                    state["base"][g] = base + bit_of(bit) * part
                else:
                    src = base
                sb[block, m, off : off + part, :] = grad[m, pl.ds(al(src, part), part), :].astype(BF)
                area = pl.ds(off, part)
                state["c"].append(
                    ctx_copy(block, m, sb.at[block, m, area], rb.at[block, m, area], t, bit)
                )

        def land(s):
            for g, (steps, _) in enumerate(groups):
                bit, halve, size, part, off, t = steps[s]
                state["c"][g].wait_recv()
                rows = pl.ds(al(state["base"][g], part), part)
                grad[m, rows, :] = grad[m, rows, :] + rb[block, m, off : off + part, :].astype(F32)

        def settle():
            for g, (_, size) in enumerate(groups):
                rows = pl.ds(al(state["base"][g], size), size)
                red[block, m, rows, :] = grad[m, rows, :].astype(BF)

        n_steps = n_bits - 1

        def return_launch(s):
            state["c"] = []
            for g, (steps, _) in enumerate(groups):
                bit, halve, size, part, off, t = steps[s]
                if not halve:
                    continue
                rows = pl.ds(al(state["base"][g], part), part)
                here = red.at[block, m, rows]
                state["c"].append(
                    ctx_copy(block, m, here, here, back_at + g * n_steps + s, bit)
                )

        def return_land(s):
            for c in state["c"]:
                c.wait_recv()
            for g, (steps, _) in enumerate(groups):
                bit, halve, size, part, off, t = steps[s]
                if halve:
                    state["base"][g] = state["base"][g] - bit_of(bit) * part

        def last_launch():
            here = red.at[block, m, pl.ds(al(mine, half), half)]
            state["c"] = [ctx_copy(block, m, here, here, back_at + 2 * n_steps, 0)]

        def last_land():
            state["c"][0].wait_recv()

        acts = [first, land_first]
        for s in range(n_steps):
            acts += [functools.partial(launch, s), functools.partial(land, s)]
        acts.append(settle)
        for s in reversed(range(n_steps)):
            acts += [functools.partial(return_launch, s), functools.partial(return_land, s)]
        acts += [last_launch, last_land]
        steps, now = [], []
        for a in acts:
            name = a.func if isinstance(a, functools.partial) else a
            now.append(a)
            if name in (first, launch, return_launch, last_launch):
                steps.append(now)
                now = []
        steps.append(now)
        return steps

    def newton_schulz(block, m):
        r = red[block, m].astype(F32)
        inv = 1.0 / (jnp.sqrt(jnp.sum(r * r, keepdims=True)) + 1e-07)
        xs[...] = (r * inv).astype(BF)
        for _ in range(NS_STEPS):
            sq[...] = dot(xs[...], xs[...], 1, 1).astype(BF)
            mx[...] = (ns_cubic * sq[...].astype(F32) + ns_quintic * dot(sq[...], sq[...])).astype(BF)
            xs[...] = (ns_linear * xs[...].astype(F32) + dot(mx[...], xs[...])).astype(BF)
        new = w32[m] + xs[...].astype(F32)
        w32[m] = new
        wb[m] = new.astype(BF)

    ORDER = (2, 0, 1)

    def run_sums(block, before, after, fillers):
        todo = []
        for i, m in enumerate(ORDER):
            for s, acts in enumerate(sum_steps(block, m)):
                todo.append((s + LAG * i if s > 0 else 0, i, s, m, acts))
            n_steps = s
        fillers = list(fillers)
        for level in range(n_steps + LAG * (len(ORDER) - 1) + 1):
            work = []
            for at, i, s, m, acts in todo:
                if at != level:
                    continue
                if s == 0:
                    before[m]()
                for a in acts:
                    a()
                if s == n_steps:
                    work.append(after[m])
            if level > 0 and fillers:
                fillers.pop(0)()
            for w in work:
                w()
        for f in fillers:
            f()

    def attend(j):
        cols = slice(j * AH, (j + 1) * AH)
        reach = win_ref[head * (fw // AH) + j]
        for i in range(count // WIN):
            q = q_all[i * WIN : (i + 1) * WIN, cols]
            keys = k_all[i * WIN : (i + 2) * WIN, cols]
            vals = v_all[i * WIN : (i + 2) * WIN, cols]
            scores = dot(q, keys, 1, 1) * (1.0 / math.sqrt(AH))
            row = lax.broadcasted_iota(jnp.int32, (WIN, 2 * WIN), 0)
            col = lax.broadcasted_iota(jnp.int32, (WIN, 2 * WIN), 1)
            gap = row + WIN - col
            allowed = (gap >= 0) & (gap < reach)
            if i == 0:
                allowed = allowed & (ctx * count - WIN + col >= 0)
            masked = jnp.where(allowed, scores, -jnp.inf)
            e = jnp.exp(masked - jnp.max(masked, axis=-1, keepdims=True))
            w = (e * (1.0 / jnp.sum(e, axis=-1, keepdims=True))).astype(BF)
            attended[i * WIN : (i + 1) * WIN, cols] = dot(w, vals).astype(BF)

    for c in locals_[:1]:
        c.wait()
    for c in k_copies:
        c.wait_recv()
    chunks(count, rms_keys)
    kbt[...] = kb[...].T
    pre_g[...] = dot(kb[...], wb[0])
    pre_u[...] = dot(kb[...], wb[1])
    make_hidden()
    locals_[1].wait()
    for c in v_copies:
        c.wait_recv()
    for c in q_copies:
        c.start()
    halos = []
    for i, ref in enumerate((k_all, v_all)):
        halos.append(
            pltpu.make_async_remote_copy(
                src_ref=ref.at[pl.ds(count, WIN)],
                dst_ref=ref.at[pl.ds(0, WIN)],
                send_sem=halo_send.at[i],
                recv_sem=halo_recv.at[i],
                device_id={"ctx": nxt},
                device_id_type=MESH,
            )
        )
    sent.extend(halos)

    def grad_down():
        grad[2] = dot(hid[...], tgt[...], 0, 0)

    def grad_gate():
        grad[0] = dot(kbt[...], bg[...])

    def grad_up():
        grad[1] = dot(kbt[...], bu[...])

    def first_gate():
        back[...] = dot(tgt[...], wb[2], 1, 1)
        make_back(False)
        grad_gate()

    def mid_down():
        newton_schulz(0, 2)
        make_target(1)
        back[...] = dot(tgt[...], wb[2], 1, 1)

    def mid_gate():
        newton_schulz(0, 0)
        pre_g[...] = dot(kb[...], wb[0])

    def mid_up():
        for c in halos:
            c.start()
        newton_schulz(0, 1)
        pre_u[...] = dot(kb[...], wb[1])
        make_back(True)

    def end_down():
        newton_schulz(1, 2)

    def end_gate():
        newton_schulz(1, 0)
        pre_g[...] = dot(qb[...], wb[0])

    def end_up():
        newton_schulz(1, 1)
        pre_u[...] = dot(qb[...], wb[1])

    def got_queries():
        locals_[2].wait()
        for c in q_copies:
            c.wait_recv()
        chunks(count, rms_queries)
        pre_g[...] = dot(qb[...], wb[0])
        pre_u[...] = dot(qb[...], wb[1])

    def early_out():
        make_hidden()
        res1[...] = dot(hid[...], wb[2])

    def attend_first():
        for c in halos:
            c.wait_recv()
        attend(0)

    def finish_rows(rows, first):
        early = jnp.concatenate([inside(first, 64, 0)] * (fw // 128), axis=1)
        r = rms(jnp.where(early, res1[rows, :], back[rows, :]))
        out_ref[rows, :] = (attended[rows, :].astype(F32) + r).astype(BF)

    make_target(0)
    run_sums(0, {2: grad_down, 0: first_gate, 1: grad_up}, {2: mid_down, 0: mid_gate, 1: mid_up}, [])
    fill = [got_queries, early_out, attend_first]
    fill += [functools.partial(attend, j) for j in range(1, fw // AH)]
    run_sums(
        1, {2: grad_down, 0: grad_gate, 1: grad_up}, {2: end_down, 0: end_gate, 1: end_up}, fill
    )
    make_hidden()
    back[...] = dot(hid[...], wb[2])
    chunks(count, finish_rows)
    for c in sent:
        c.wait_send()


def local(attn_q, attn_k, attn_v, step_size, fast_init, boundary, window_len):
    n_ctx = lax.axis_size("ctx")
    n_head = lax.axis_size("head")
    tok, width = attn_q.shape
    fw = width // n_head
    count = tok * n_head
    _, staged, _, transfers = sum_plan(fw, n_ctx.bit_length() - 1)
    hbm = pl.BlockSpec(memory_space=pltpu.HBM)
    vmem = pl.BlockSpec(memory_space=pltpu.VMEM)
    smem = pl.BlockSpec(memory_space=pltpu.SMEM)
    big = lambda dtype, *lead: pltpu.VMEM(lead + (count, fw), dtype)
    mat = lambda dtype, *lead: pltpu.VMEM(lead + (fw, fw), dtype)
    return pl.pallas_call(
        functools.partial(kernel, n_ctx, n_head),
        out_shape=jax.ShapeDtypeStruct((count, fw), BF),
        in_specs=[hbm, hbm, hbm, vmem, hbm, smem, smem],
        out_specs=vmem,
        scratch_shapes=[
            big(BF),
            pltpu.VMEM((count + WIN, fw), BF),
            pltpu.VMEM((count + WIN, fw), BF),
            big(BF),
            pltpu.VMEM((fw, count), BF),
            big(BF),
            pltpu.VMEM((count, 128), F32),
            mat(F32, 3),
            mat(BF, 3),
            big(F32),
            big(F32),
            big(F32),
            big(BF),
            big(BF),
            big(BF),
            big(BF),
            mat(BF),
            mat(BF),
            mat(BF),
            mat(F32, 3),
            big(BF),
            big(F32),
            pltpu.VMEM((2, 3, staged, fw), BF),
            pltpu.VMEM((2, 3, staged, fw), BF),
            mat(BF, 2, 3),
            pltpu.SemaphoreType.DMA((4,)),
            pltpu.SemaphoreType.DMA((3, n_head - 1)),
            pltpu.SemaphoreType.DMA((3, n_head - 1)),
            pltpu.SemaphoreType.DMA((2,)),
            pltpu.SemaphoreType.DMA((2,)),
            pltpu.SemaphoreType.DMA((2, 3, transfers)),
            pltpu.SemaphoreType.DMA((2, 3, transfers)),
        ],
        compiler_params=pltpu.CompilerParams(
            collective_id=0, has_side_effects=True, vmem_limit_bytes=60 * 1024 * 1024
        ),
    )(attn_q, attn_k, attn_v, step_size, fast_init, boundary, window_len)


def solution(mesh):
    return jax.shard_map(
        local,
        mesh=mesh,
        in_specs=(
            P(("ctx", "head"), None),
            P(("ctx", "head"), None),
            P(("ctx", "head"), None),
            P("head", "ctx"),
            P("head", None, None, None),
            P(),
            P(),
        ),
        out_specs=P("ctx", "head"),
        check_vma=False,
    )
```

profile of v0, /device:TPU:9, one launch (start us, length us, event | category | flops | bytes accessed | tf_op | source)
XLA Modules:
  0.0 94.0 jit_solution(580605271882454320)
XLA Ops:
  0.7 91.4 %shard_map.73 = bf16[512,512]{1,0:T(8,128)(2,1)} custom-call(bf16[128,2048]{1,0:T(8,128)(2,1)} %q_hbm.1, bf16[128,2048]{1,0:T(8,128)(2,1)} %k_hbm.1, bf16[128,2048]{1,0:T(8,128)(2,1)} %v_hbm.1, f32[1,512]{1,0:T(1,128)} %step_ref.1, f32[1,3,512,512]{3,2,1,0:T(8,128)} %init_hbm.1, s32[1]{0:T(128)S(6)} %copy.9.bound_ref, s32[16]{0:T(128)} %win_ref.1), custom_call_target="tpu_custom_call" | custom-call | tf_op jit(solution)/shard_map/pallas_call | solution.py:465
  92.1 1.9 %copy.10 = bf16[512,512]{1,0:T(8,128)(2,1)} copy(bf16[512,512]{1,0:T(8,128)(2,1)} %shard_map.73) | data formatting | bytes 1048576
where the time goes:
time: 95.3 us; the launch traced here: 94 us
  Pallas kernels  91.4 us (96%)
  local copies, waits for them, and re-layouts  1.87 us (2%)
    pallas_call x1, Pallas kernels, local(): pl.pallas_call(functools.partial(kernel, n_ctx, n_head), out_shape=jax.Sh...  91.4 us

commit v1 on v0

--- a/solution.py
+++ b/solution.py
@@ -43,10 +43,10 @@
 
 
 def kernel(
-    n_ctx, n_head, q_hbm, k_hbm, v_hbm, step_ref, init_hbm, bound_ref, win_ref, out_ref,
-    q_all, k_all, v_all, kb, kbt, qb, step_t, w32, wb, pre_g, pre_u, back, hid, tgt, bg, bu, xs, sq, mx,
-    grad, attended, res1, sb, rb, red,
-    loc_sem, a2a_send, a2a_recv, halo_send, halo_recv, ar_send, ar_recv,
+    n_ctx, n_head, q_hbm, k_hbm, v_hbm, step_hbm, init_hbm, bound_hbm, win_hbm, out_ref,
+    q_all, k_all, v_all, kb, kbt, qb, step_t, w32, wb, pre, back, hid, tgt, bg, bu, xs, sq, mx,
+    grad, attended, res1, sb, rb, red, x_out, x_in, step_ref, bound_ref, win_ref,
+    loc_sem, a2a_send, a2a_recv, halo_send, halo_recv, ar_send, ar_recv, x_send, x_recv,
 ):
     ctx = lax.axis_index("ctx")
     head = lax.axis_index("head")
@@ -88,6 +88,14 @@
     for c in locals_:
         c.start()
     init_copy.start()
+    small = [
+        pltpu.make_async_copy(src, dst, loc_sem.at[4 + i])
+        for i, (src, dst) in enumerate(
+            ((step_hbm, step_ref), (bound_hbm, bound_ref), (win_hbm, win_ref))
+        )
+    ]
+    for c in small:
+        c.start()
 
     pl.semaphore_wait(barrier, n_head - 1 + n_bits + 2)
 
@@ -116,6 +124,8 @@
         c.start()
     sent = k_copies + v_copies + q_copies
 
+    for c in small:
+        c.wait()
     for i in range(count // 128):
         wide = jnp.broadcast_to(step_ref[0:1, i * 128 : (i + 1) * 128], (128, 128))
         step_t[i * 128 : (i + 1) * 128, :] = wide.T
@@ -159,8 +169,8 @@
 
     def make_hidden():
         def body(rows, first):
-            g = pre_g[rows, :]
-            u = pre_u[rows, :]
+            g = pre[0, rows, :]
+            u = pre[1, rows, :]
             act = g * jax.nn.sigmoid(g)
             hid[rows, :] = (act * u).astype(BF)
 
@@ -168,8 +178,8 @@
 
     def make_back(with_hidden):
         def body(rows, first):
-            g = pre_g[rows, :]
-            u = pre_u[rows, :]
+            g = pre[0, rows, :]
+            u = pre[1, rows, :]
             o = back[rows, :]
             sig = jax.nn.sigmoid(g)
             act = g * sig
@@ -267,6 +277,11 @@
             here = red.at[block, m, pl.ds(al(mine, half), half)]
             state["c"] = [ctx_copy(block, m, here, here, back_at + 2 * n_steps, 0)]
 
+        def joint_launch():
+            theirs = 1 - bit_of(0)
+            here = red.at[block, theirs, pl.ds(al(mine, half), half)]
+            state["c"] = [ctx_copy(block, m, here, here, back_at + 2 * n_steps, 0)]
+
         def last_land():
             state["c"][0].wait_recv()
 
@@ -276,39 +291,71 @@
         acts.append(settle)
         for s in reversed(range(n_steps)):
             acts += [functools.partial(return_launch, s), functools.partial(return_land, s)]
-        acts += [last_launch, last_land]
+        if m == 2:
+            acts += [last_launch, last_land]
+        elif m == 1:
+            acts += [joint_launch, last_land]
         steps, now = [], []
         for a in acts:
             name = a.func if isinstance(a, functools.partial) else a
             now.append(a)
-            if name in (first, launch, return_launch, last_launch):
+            if name in (first, launch, return_launch, last_launch, joint_launch):
                 steps.append(now)
                 now = []
         steps.append(now)
         return steps
 
-    def newton_schulz(block, m):
+    def newton_schulz(block, m, out):
         r = red[block, m].astype(F32)
         inv = 1.0 / (jnp.sqrt(jnp.sum(r * r, keepdims=True)) + 1e-07)
         xs[...] = (r * inv).astype(BF)
-        for _ in range(NS_STEPS):
+        for step in range(NS_STEPS):
             sq[...] = dot(xs[...], xs[...], 1, 1).astype(BF)
             mx[...] = (ns_cubic * sq[...].astype(F32) + ns_quintic * dot(sq[...], sq[...])).astype(BF)
-            xs[...] = (ns_linear * xs[...].astype(F32) + dot(mx[...], xs[...])).astype(BF)
-        new = w32[m] + xs[...].astype(F32)
+            x = (ns_linear * xs[...].astype(F32) + dot(mx[...], xs[...])).astype(BF)
+            if step < NS_STEPS - 1:
+                xs[...] = x
+            else:
+                out[...] = x
+
+    def add_update(m, x):
+        new = w32[m] + x[...].astype(F32)
         w32[m] = new
         wb[m] = new.astype(BF)
 
+    def down_update(block):
+        newton_schulz(block, 2, xs)
+        add_update(2, xs)
+
+    def pair_update(block, rows_in):
+        own = bit_of(0)
+        newton_schulz(block, own, x_out.at[block])
+        c = pltpu.make_async_remote_copy(
+            src_ref=x_out.at[block],
+            dst_ref=x_in.at[block],
+            send_sem=x_send.at[block],
+            recv_sem=x_recv.at[block],
+            device_id={"ctx": partner(0)},
+            device_id_type=MESH,
+        )
+        c.start()
+        sent.append(c)
+        add_update(own, x_out.at[block])
+        pre[own] = dot(rows_in[...], wb[own])
+        c.wait_recv()
+        add_update(1 - own, x_in.at[block])
+        pre[1 - own] = dot(rows_in[...], wb[1 - own])
+
     ORDER = (2, 0, 1)
 
     def run_sums(block, before, after, fillers):
-        todo = []
+        todo, n_steps = [], 0
         for i, m in enumerate(ORDER):
             for s, acts in enumerate(sum_steps(block, m)):
-                todo.append((s + LAG * i if s > 0 else 0, i, s, m, acts))
-            n_steps = s
+                todo.append((s + LAG * min(i, 1) if s > 0 else 0, i, s, m, acts))
+                n_steps = max(s, n_steps)
         fillers = list(fillers)
-        for level in range(n_steps + LAG * (len(ORDER) - 1) + 1):
+        for level in range(n_steps + LAG + 1):
             work = []
             for at, i, s, m, acts in todo:
                 if at != level:
@@ -317,7 +364,7 @@
                     before[m]()
                 for a in acts:
                     a()
-                if s == n_steps:
+                if s == n_steps and m in after:
                     work.append(after[m])
             if level > 0 and fillers:
                 fillers.pop(0)()
@@ -351,8 +398,8 @@
         c.wait_recv()
     chunks(count, rms_keys)
     kbt[...] = kb[...].T
-    pre_g[...] = dot(kb[...], wb[0])
-    pre_u[...] = dot(kb[...], wb[1])
+    pre[0] = dot(kb[...], wb[0])
+    pre[1] = dot(kb[...], wb[1])
     make_hidden()
     locals_[1].wait()
     for c in v_copies:
@@ -388,39 +435,29 @@
         grad_gate()
 
     def mid_down():
-        newton_schulz(0, 2)
+        down_update(0)
         make_target(1)
         back[...] = dot(tgt[...], wb[2], 1, 1)
 
-    def mid_gate():
-        newton_schulz(0, 0)
-        pre_g[...] = dot(kb[...], wb[0])
-
-    def mid_up():
+    def mid_pair():
         for c in halos:
             c.start()
-        newton_schulz(0, 1)
-        pre_u[...] = dot(kb[...], wb[1])
+        pair_update(0, kb)
         make_back(True)
 
     def end_down():
-        newton_schulz(1, 2)
-
-    def end_gate():
-        newton_schulz(1, 0)
-        pre_g[...] = dot(qb[...], wb[0])
-
-    def end_up():
-        newton_schulz(1, 1)
-        pre_u[...] = dot(qb[...], wb[1])
+        down_update(1)
+
+    def end_pair():
+        pair_update(1, qb)
 
     def got_queries():
         locals_[2].wait()
         for c in q_copies:
             c.wait_recv()
         chunks(count, rms_queries)
-        pre_g[...] = dot(qb[...], wb[0])
-        pre_u[...] = dot(qb[...], wb[1])
+        pre[0] = dot(qb[...], wb[0])
+        pre[1] = dot(qb[...], wb[1])
 
     def early_out():
         make_hidden()
@@ -437,11 +474,11 @@
         out_ref[rows, :] = (attended[rows, :].astype(F32) + r).astype(BF)
 
     make_target(0)
-    run_sums(0, {2: grad_down, 0: first_gate, 1: grad_up}, {2: mid_down, 0: mid_gate, 1: mid_up}, [])
+    run_sums(0, {2: grad_down, 0: first_gate, 1: grad_up}, {2: mid_down, 1: mid_pair}, [])
     fill = [got_queries, early_out, attend_first]
     fill += [functools.partial(attend, j) for j in range(1, fw // AH)]
     run_sums(
-        1, {2: grad_down, 0: grad_gate, 1: grad_up}, {2: end_down, 0: end_gate, 1: end_up}, fill
+        1, {2: grad_down, 0: grad_gate, 1: grad_up}, {2: end_down, 1: end_pair}, fill
     )
     make_hidden()
     back[...] = dot(hid[...], wb[2])
@@ -459,13 +496,12 @@
     _, staged, _, transfers = sum_plan(fw, n_ctx.bit_length() - 1)
     hbm = pl.BlockSpec(memory_space=pltpu.HBM)
     vmem = pl.BlockSpec(memory_space=pltpu.VMEM)
-    smem = pl.BlockSpec(memory_space=pltpu.SMEM)
     big = lambda dtype, *lead: pltpu.VMEM(lead + (count, fw), dtype)
     mat = lambda dtype, *lead: pltpu.VMEM(lead + (fw, fw), dtype)
     return pl.pallas_call(
         functools.partial(kernel, n_ctx, n_head),
         out_shape=jax.ShapeDtypeStruct((count, fw), BF),
-        in_specs=[hbm, hbm, hbm, vmem, hbm, smem, smem],
+        in_specs=[hbm] * 7,
         out_specs=vmem,
         scratch_shapes=[
             big(BF),
@@ -477,8 +513,7 @@
             pltpu.VMEM((count, 128), F32),
             mat(F32, 3),
             mat(BF, 3),
-            big(F32),
-            big(F32),
+            big(F32, 2),
             big(F32),
             big(BF),
             big(BF),
@@ -493,13 +528,20 @@
             pltpu.VMEM((2, 3, staged, fw), BF),
             pltpu.VMEM((2, 3, staged, fw), BF),
             mat(BF, 2, 3),
-            pltpu.SemaphoreType.DMA((4,)),
+            mat(BF, 2),
+            mat(BF, 2),
+            pltpu.VMEM(step_size.shape, F32),
+            pltpu.SMEM(boundary.shape, jnp.int32),
+            pltpu.SMEM(window_len.shape, jnp.int32),
+            pltpu.SemaphoreType.DMA((7,)),
             pltpu.SemaphoreType.DMA((3, n_head - 1)),
             pltpu.SemaphoreType.DMA((3, n_head - 1)),
             pltpu.SemaphoreType.DMA((2,)),
             pltpu.SemaphoreType.DMA((2,)),
             pltpu.SemaphoreType.DMA((2, 3, transfers)),
             pltpu.SemaphoreType.DMA((2, 3, transfers)),
+            pltpu.SemaphoreType.DMA((2,)),
+            pltpu.SemaphoreType.DMA((2,)),
         ],
         compiler_params=pltpu.CompilerParams(
             collective_id=0, has_side_effects=True, vmem_limit_bytes=60 * 1024 * 1024

time: 95.3 us -> 91.7 us (0.962); the launches traced: 94 us -> 91.5 us
  Pallas kernels: 91.4 us -> 89 us
    pallas_call x1, Pallas kernels: 91.4 us -> 89 us  [local(): pl.pallas_call(functools.partial(kernel, n_ctx, n_head), out_shape=jax.Sh...]
where the time goes in v1:
time: 91.7 us; the launch traced here: 91.5 us
  Pallas kernels  89 us (97%)
  local copies, waits for them, and re-layouts  1.87 us (2%)
    pallas_call x1, Pallas kernels, local(): pl.pallas_call(functools.partial(kernel, n_ctx, n_head), out_shape=jax.Sh...  89 us
    unnamed x1, local copies, waits for them, and re-layouts  1.87 us

profile of v1, /device:TPU:9, one launch (start us, length us, event | category | flops | bytes accessed | tf_op | source)
XLA Modules:
  0.0 91.5 jit_solution(14391250975777111656)
XLA Ops:
  0.7 89.0 %shard_map.73 = bf16[512,512]{1,0:T(8,128)(2,1)} custom-call(bf16[128,2048]{1,0:T(8,128)(2,1)} %q_hbm.1, bf16[128,2048]{1,0:T(8,128)(2,1)} %k_hbm.1, bf16[128,2048]{1,0:T(8,128)(2,1)} %v_hbm.1, f32[1,512]{1,0:T(1,128)} %step_hbm.1, f32[1,3,512,512]{3,2,1,0:T(8,128)} %init_hbm.1, s32[1]{0:T(128)S(6)} %copy.9.bound_hbm, s32[16]{0:T(128)} %win_hbm.1), custom_call_target="tpu_custom_call" | custom-call | tf_op jit(solution)/shard_map/pallas_call | solution.py:501
  89.6 1.9 %copy.10 = bf16[512,512]{1,0:T(8,128)(2,1)} copy(bf16[512,512]{1,0:T(8,128)(2,1)} %shard_map.73) | data formatting | bytes 1048576

commit v2 on v1

--- a/solution.py
+++ b/solution.py
@@ -167,11 +167,14 @@
 
         chunks(count, body)
 
+    def sigmoid(x):
+        return 0.5 * jnp.tanh(0.5 * x) + 0.5
+
     def make_hidden():
         def body(rows, first):
             g = pre[0, rows, :]
             u = pre[1, rows, :]
-            act = g * jax.nn.sigmoid(g)
+            act = g * sigmoid(g)
             hid[rows, :] = (act * u).astype(BF)
 
         chunks(count, body)
@@ -181,7 +184,7 @@
             g = pre[0, rows, :]
             u = pre[1, rows, :]
             o = back[rows, :]
-            sig = jax.nn.sigmoid(g)
+            sig = sigmoid(g)
             act = g * sig
             if with_hidden:
                 hid[rows, :] = (act * u).astype(BF)
@@ -305,44 +308,58 @@
         steps.append(now)
         return steps
 
-    def newton_schulz(block, m, out):
+    def ns_step(out, rows_done=None):
+        sq[...] = dot(xs[...], xs[...], 1, 1).astype(BF)
+        mx[...] = (ns_cubic * sq[...].astype(F32) + ns_quintic * dot(sq[...], sq[...])).astype(BF)
+        if rows_done is None:
+            out[...] = (ns_linear * xs[...].astype(F32) + dot(mx[...], xs[...])).astype(BF)
+        else:
+            for i in range(2):
+                rows = slice(i * half, (i + 1) * half)
+                out[rows, :] = (
+                    ns_linear * xs[rows, :].astype(F32) + dot(mx[rows, :], xs[...])
+                ).astype(BF)
+                rows_done(i)
+
+    def ns_start(block, m):
         r = red[block, m].astype(F32)
         inv = 1.0 / (jnp.sqrt(jnp.sum(r * r, keepdims=True)) + 1e-07)
         xs[...] = (r * inv).astype(BF)
-        for step in range(NS_STEPS):
-            sq[...] = dot(xs[...], xs[...], 1, 1).astype(BF)
-            mx[...] = (ns_cubic * sq[...].astype(F32) + ns_quintic * dot(sq[...], sq[...])).astype(BF)
-            x = (ns_linear * xs[...].astype(F32) + dot(mx[...], xs[...])).astype(BF)
-            if step < NS_STEPS - 1:
-                xs[...] = x
-            else:
-                out[...] = x
+        for _ in range(NS_STEPS - 1):
+            ns_step(xs)
 
     def add_update(m, x):
         new = w32[m] + x[...].astype(F32)
         w32[m] = new
         wb[m] = new.astype(BF)
 
-    def down_update(block):
-        newton_schulz(block, 2, xs)
+    def down_update():
+        ns_step(xs)
         add_update(2, xs)
 
     def pair_update(block, rows_in):
         own = bit_of(0)
-        newton_schulz(block, own, x_out.at[block])
-        c = pltpu.make_async_remote_copy(
-            src_ref=x_out.at[block],
-            dst_ref=x_in.at[block],
-            send_sem=x_send.at[block],
-            recv_sem=x_recv.at[block],
-            device_id={"ctx": partner(0)},
-            device_id_type=MESH,
-        )
-        c.start()
-        sent.append(c)
+        copies = []
+
+        def rows_done(i):
+            c = pltpu.make_async_remote_copy(
+                src_ref=x_out.at[block, pl.ds(i * half, half)],
+                dst_ref=x_in.at[block, pl.ds(i * half, half)],
+                send_sem=x_send.at[block, i],
+                recv_sem=x_recv.at[block, i],
+                device_id={"ctx": partner(0)},
+                device_id_type=MESH,
+            )
+            c.start()
+            copies.append(c)
+
+        ns_start(block, own)
+        ns_step(x_out.at[block], rows_done)
+        sent.extend(copies)
         add_update(own, x_out.at[block])
         pre[own] = dot(rows_in[...], wb[own])
-        c.wait_recv()
+        for c in copies:
+            c.wait_recv()
         add_update(1 - own, x_in.at[block])
         pre[1 - own] = dot(rows_in[...], wb[1 - own])
 
@@ -365,6 +382,8 @@
                 for a in acts:
                     a()
                 if s == n_steps and m in after:
+                    if m == 2:
+                        ns_start(block, m)
                     work.append(after[m])
             if level > 0 and fillers:
                 fillers.pop(0)()
@@ -435,7 +454,7 @@
         grad_gate()
 
     def mid_down():
-        down_update(0)
+        down_update()
         make_target(1)
         back[...] = dot(tgt[...], wb[2], 1, 1)
 
@@ -446,7 +465,7 @@
         make_back(True)
 
     def end_down():
-        down_update(1)
+        down_update()
 
     def end_pair():
         pair_update(1, qb)
@@ -540,8 +559,8 @@
             pltpu.SemaphoreType.DMA((2,)),
             pltpu.SemaphoreType.DMA((2, 3, transfers)),
             pltpu.SemaphoreType.DMA((2, 3, transfers)),
-            pltpu.SemaphoreType.DMA((2,)),
-            pltpu.SemaphoreType.DMA((2,)),
+            pltpu.SemaphoreType.DMA((2, 2)),
+            pltpu.SemaphoreType.DMA((2, 2)),
         ],
         compiler_params=pltpu.CompilerParams(
             collective_id=0, has_side_effects=True, vmem_limit_bytes=60 * 1024 * 1024

time: 91.7 us -> 89 us (0.971)
  Pallas kernels: 89 us -> 86.3 us
    pallas_call x1, Pallas kernels: 89 us -> 86.3 us  [local(): pl.pallas_call(functools.partial(kernel, n_ctx, n_head), out_shape=jax.Sh...]
where the time goes in v2:
time: 89 us; the launch traced here: 88.9 us
  Pallas kernels  86.3 us (97%)
  local copies, waits for them, and re-layouts  1.87 us (2%)
    pallas_call x1, Pallas kernels, local(): pl.pallas_call(functools.partial(kernel, n_ctx, n_head), out_shape=jax.Sh...  86.3 us
    unnamed x1, local copies, waits for them, and re-layouts  1.87 us

profile of v2, /device:TPU:9, one launch (start us, length us, event | category | flops | bytes accessed | tf_op | source)
XLA Modules:
  0.0 88.9 jit_solution(4588921113456705187)
XLA Ops:
  0.7 86.3 %shard_map.73 = bf16[512,512]{1,0:T(8,128)(2,1)} custom-call(bf16[128,2048]{1,0:T(8,128)(2,1)} %q_hbm.1, bf16[128,2048]{1,0:T(8,128)(2,1)} %k_hbm.1, bf16[128,2048]{1,0:T(8,128)(2,1)} %v_hbm.1, f32[1,512]{1,0:T(1,128)} %step_hbm.1, f32[1,3,512,512]{3,2,1,0:T(8,128)} %init_hbm.1, s32[1]{0:T(128)S(6)} %copy.9.bound_hbm, s32[16]{0:T(128)} %win_hbm.1), custom_call_target="tpu_custom_call" | custom-call | tf_op jit(solution)/shard_map/pallas_call | solution.py:520
  87.0 1.9 %copy.10 = bf16[512,512]{1,0:T(8,128)(2,1)} copy(bf16[512,512]{1,0:T(8,128)(2,1)} %shard_map.73) | data formatting | bytes 1048576

commit v3 on v2

--- a/solution.py
+++ b/solution.py
@@ -385,17 +385,18 @@
                     if m == 2:
                         ns_start(block, m)
                     work.append(after[m])
-            if level > 0 and fillers:
-                fillers.pop(0)()
+            f = fillers.pop(0) if level > 0 and fillers else None
+            if f is not None:
+                f()
             for w in work:
                 w()
         for f in fillers:
             f()
 
-    def attend(j):
+    def attend(j, blocks):
         cols = slice(j * AH, (j + 1) * AH)
         reach = win_ref[head * (fw // AH) + j]
-        for i in range(count // WIN):
+        for i in blocks:
             q = q_all[i * WIN : (i + 1) * WIN, cols]
             keys = k_all[i * WIN : (i + 2) * WIN, cols]
             vals = v_all[i * WIN : (i + 2) * WIN, cols]
@@ -455,7 +456,6 @@
 
     def mid_down():
         down_update()
-        make_target(1)
         back[...] = dot(tgt[...], wb[2], 1, 1)
 
     def mid_pair():
@@ -470,11 +470,20 @@
     def end_pair():
         pair_update(1, qb)
 
+    n_heads = fw // AH
+
+    def inner_rows(heads):
+        for j in heads:
+            attend(j, range(1, count // WIN))
+
     def got_queries():
         locals_[2].wait()
         for c in q_copies:
             c.wait_recv()
         chunks(count, rms_queries)
+        inner_rows(range(n_heads // 2))
+
+    def early_pre():
         pre[0] = dot(qb[...], wb[0])
         pre[1] = dot(qb[...], wb[1])
 
@@ -485,7 +494,8 @@
     def attend_first():
         for c in halos:
             c.wait_recv()
-        attend(0)
+        for j in range(n_heads):
+            attend(j, range(1))
 
     def finish_rows(rows, first):
         early = jnp.concatenate([inside(first, 64, 0)] * (fw // 128), axis=1)
@@ -493,9 +503,15 @@
         out_ref[rows, :] = (attended[rows, :].astype(F32) + r).astype(BF)
 
     make_target(0)
-    run_sums(0, {2: grad_down, 0: first_gate, 1: grad_up}, {2: mid_down, 1: mid_pair}, [])
-    fill = [got_queries, early_out, attend_first]
-    fill += [functools.partial(attend, j) for j in range(1, fw // AH)]
+    fill = [
+        functools.partial(make_target, 1),
+        None,
+        None,
+        got_queries,
+        functools.partial(inner_rows, range(n_heads // 2, n_heads)),
+    ]
+    run_sums(0, {2: grad_down, 0: first_gate, 1: grad_up}, {2: mid_down, 1: mid_pair}, fill)
+    fill = [early_pre, early_out, attend_first]
     run_sums(
         1, {2: grad_down, 0: grad_gate, 1: grad_up}, {2: end_down, 1: end_pair}, fill
     )

time: 89 us -> 88.5 us (level)
  no operation moved by 1% of the time
where the time goes in v3:
time: 88.5 us; the launch traced here: 88.3 us
  Pallas kernels  85.8 us (97%)
  local copies, waits for them, and re-layouts  1.87 us (2%)
    pallas_call x1, Pallas kernels, local(): pl.pallas_call(functools.partial(kernel, n_ctx, n_head), out_shape=jax.Sh...  85.8 us
    unnamed x1, local copies, waits for them, and re-layouts  1.87 us

profile of v3, /device:TPU:9, one launch (start us, length us, event | category | flops | bytes accessed | tf_op | source)
XLA Modules:
  0.0 88.3 jit_solution(2954014166140105916)
XLA Ops:
  0.7 85.8 %shard_map.73 = bf16[512,512]{1,0:T(8,128)(2,1)} custom-call(bf16[128,2048]{1,0:T(8,128)(2,1)} %q_hbm.1, bf16[128,2048]{1,0:T(8,128)(2,1)} %k_hbm.1, bf16[128,2048]{1,0:T(8,128)(2,1)} %v_hbm.1, f32[1,512]{1,0:T(1,128)} %step_hbm.1, f32[1,3,512,512]{3,2,1,0:T(8,128)} %init_hbm.1, s32[1]{0:T(128)S(6)} %copy.9.bound_hbm, s32[16]{0:T(128)} %win_hbm.1), custom_call_target="tpu_custom_call" | custom-call | tf_op jit(solution)/shard_map/pallas_call | solution.py:536
  86.4 1.9 %copy.10 = bf16[512,512]{1,0:T(8,128)(2,1)} copy(bf16[512,512]{1,0:T(8,128)(2,1)} %shard_map.73) | data formatting | bytes 1048576
